TPU v7x, 128 devices: a whole 4x4x4 slice. The times are simulated.
128 devices in a mesh: cam: 32 (over z, x, core), trk: 4 (over y).
Axes of the slice: x: 4, y: 4, z: 4, core: 2. Of those that a mesh axis runs over, the one named last changes fastest.
Arguments:
- grad_cam: float32 [128, 768], P('cam'), may hold values from -6 to 6
- cam_diag: float32 [128, 768], P('cam'), may hold values from 4 to 8
- precond: float32 [128, 768], P('cam'), may hold values from 0.12 to 0.3
- point_inv: float32 [2048, 9, 128], P(('cam', 'trk')), may hold values from -0.15 to 1.2, as said below
- tiles: bfloat16 [3072, 768, 384], P(('cam', 'trk')), may hold values from -0.0234375 to 0.0234375
- tile_block: int32 [3072], P(('cam', 'trk')), may hold values from 0 to 3
- tile_owner: int32 [3072], P(('cam', 'trk')), may hold values from 0 to 31, as said below
- tile_track: int32 [3072], P(('cam', 'trk')), may hold values from 0 to 15, as said below
- tile_live: int32 [128], P(('cam', 'trk')), may hold values from 6 to 24, as said below
- covis: bfloat16 [512, 768, 768], P(('cam', 'trk')), may hold values from -0.0546875 to 0.0546875
- pair_row: int32 [512], P(('cam', 'trk')), may hold values from 0 to 3
- pair_col: int32 [512], P(('cam', 'trk')), may hold values from 0 to 127, as said below
Outputs:
- step_field: float32 [128, 768], P('cam')
- residual: float32 [128, 768], P('cam')
Inputs may be any that keep to these rules, and one draw needn't show every extreme that they name: `tile_owner`: at most 4 tiles of one device name one owner, and on every device some owner is named by exactly 4 of its live tiles. `tile_track`: no two tiles of one device name the same owner and track tile. `tile_live`: some device has all 24 tiles live. `pair_col`: A pair's two camera blocks differ. `point_inv`: each point's block is symmetric positive definite.
All inputs are finite; a program needn't handle non-finite values.
Results may differ from a plain program's by a relative error of at most 0.0035.
Values may be sent and summed in bfloat16 or wider, within the bound.
A program may use at most 64 MiB of HBM per device.

v0:
```python
import jax
import jax.numpy as jnp
from jax import lax
from jax.sharding import PartitionSpec as P

ITERS = 2


highest = lax.Precision.HIGHEST


def invert_points(point_inv, owned_sums):
    count = owned_sums.shape[0]
    coords = owned_sums.reshape(count, 3, -1)
    blocks = point_inv.reshape(count, 3, 3, -1)
    return jnp.sum(blocks * coords[:, None, :, :], axis=2).reshape(count, -1)


def shards(
    grad_cam,
    cam_diag,
    precond,
    point_inv,
    tiles,
    tile_block,
    tile_owner,
    tile_track,
    tile_live,
    covis,
    pair_row,
    pair_col,
):
    blocks_dev = grad_cam.shape[0]
    count_tiles = tiles.shape[0]
    own_tracks = point_inv.shape[0]
    cam_count = lax.axis_size("cam")
    all_blocks = blocks_dev * cam_count
    live_mask = (jnp.arange(count_tiles) < tile_live[0]).astype(jnp.float32)
    block_hot = (tile_block[:, None] == jnp.arange(blocks_dev)[None, :]).astype(jnp.float32)
    block_pick = block_hot.astype(jnp.bfloat16)
    block_add = block_hot * live_mask[:, None]
    row_hot = (pair_row[:, None] == jnp.arange(blocks_dev)[None, :]).astype(jnp.float32)
    col_hot = (pair_col[:, None] == jnp.arange(all_blocks)[None, :]).astype(jnp.float32)
    row_pick = row_hot.astype(jnp.bfloat16)
    col_pick = col_hot.astype(jnp.bfloat16)
    dense_ids = tile_owner * own_tracks + tile_track
    dense_hot = (dense_ids[:, None] == jnp.arange(cam_count * own_tracks)[None, :]).astype(
        jnp.float32
    ) * live_mask[:, None]
    dense_pick = dense_hot.astype(jnp.bfloat16)

    def scaled_inner(residual, scaled):
        return lax.psum(jnp.sum(residual * scaled), "cam")

    step_field = jnp.zeros_like(grad_cam)
    residual = grad_cam
    scaled = precond * residual
    direction = scaled
    inner_now = scaled_inner(residual, scaled)
    for step in range(ITERS):
        rounded = direction.astype(jnp.bfloat16)
        picked_rows = jnp.dot(block_pick, rounded, preferred_element_type=jnp.float32).astype(
            jnp.bfloat16
        )
        partial_terms = jnp.einsum(
            "tk,tkq->tq", picked_rows, tiles, preferred_element_type=jnp.float32
        )
        dense_sums = jnp.dot(dense_hot.T, partial_terms, precision=highest)
        owned_sums = lax.psum_scatter(
            dense_sums.astype(jnp.bfloat16), "cam", scatter_dimension=0, tiled=True
        ).astype(jnp.float32)
        point_values = invert_points(point_inv, owned_sums).astype(jnp.bfloat16)
        every_value = lax.all_gather(point_values, "cam", axis=0, tiled=True)
        returned_vals = jnp.dot(dense_pick, every_value, preferred_element_type=jnp.float32).astype(
            jnp.bfloat16
        )
        tile_images = jnp.einsum(
            "tq,tkq->tk", returned_vals, tiles, preferred_element_type=jnp.float32
        )
        schur = jnp.dot(block_add.T, tile_images, precision=highest)
        everyone = lax.all_gather(rounded, "cam", axis=0, tiled=True)
        col_vectors = jnp.dot(col_pick, everyone, preferred_element_type=jnp.float32).astype(
            jnp.bfloat16
        )
        row_vectors = jnp.dot(row_pick, rounded, preferred_element_type=jnp.float32).astype(
            jnp.bfloat16
        )
        forward = jnp.einsum("pk,pjk->pj", col_vectors, covis, preferred_element_type=jnp.float32)
        mirrored = jnp.einsum("pj,pjk->pk", row_vectors, covis, preferred_element_type=jnp.float32)
        coupled_rows = jnp.dot(row_hot.T, forward, precision=highest)
        mirror_all = jnp.dot(col_hot.T, mirrored, precision=highest)
        mirror_own = lax.psum_scatter(
            mirror_all.astype(jnp.bfloat16), "cam", scatter_dimension=0, tiled=True
        ).astype(jnp.float32)
        summed = lax.psum(coupled_rows + mirror_own - schur, "trk")
        image = cam_diag * direction + summed
        alpha = inner_now / lax.psum(jnp.sum(direction * image), "cam")
        step_field = step_field + alpha * direction
        residual = residual - alpha * image
        scaled = precond * residual
        inner_next = scaled_inner(residual, scaled)
        direction = scaled + inner_next / inner_now * direction
        inner_now = inner_next
    return (step_field, residual)


def solution(mesh):
    in_specs = (
        P("cam", None),
        P("cam", None),
        P("cam", None),
        P(("cam", "trk"), None, None),
        P(("cam", "trk"), None, None),
        P(("cam", "trk")),
        P(("cam", "trk")),
        P(("cam", "trk")),
        P(("cam", "trk")),
        P(("cam", "trk"), None, None),
        P(("cam", "trk")),
        P(("cam", "trk")),
    )
    out_specs = (P("cam", None), P("cam", None))
    return jax.shard_map(shards, mesh=mesh, in_specs=in_specs, out_specs=out_specs, check_vma=False)
```

profile of v0, /device:TPU:1, one launch (start us, length us, event | category | flops | bytes accessed | tf_op | source)
XLA Modules:
  0.0 675.1 jit_solution(8696805639988982723)
XLA Ops:
  8.8 3.1 fusion.51
  11.9 1.8 convolution_convert_fusion.3
  15.3 7.0 %fusion.16 = f32[24,1,384]{2,1,0:T(1,128)S(1)} fusion(bf16[24,768,384]{2,1,0:T(8,128)(2,1)} %param.16, bf16[24,768,1]{1,0,2:T(8,128)(2,1)S(1)} %fusion), kind=kOutput, calls=%fused_computation.33 | convolution fusion | flops 14155776 | bytes 14229504 | tf_op jit(solution)/shard_map/tk,tkq->tq/dot_general | solution.py:65
  22.3 1.6 convolution_convert_fusion.1
  24.0 27.4 %all-gather = bf16[32,4,768]{2,1,0:T(4,128)(2,1)S(1)} all-gather(bf16[1,4,768]{2,1,0:T(4,128)(2,1)S(1)} %get-tuple-element.11), channel_id=1, replica_groups=mesh['cam'=32,'trk'=4] {'cam'}, dimensions={0}, use_global_device_ids=true | all-gather | bytes 202752 | tf_op jit(solution)/shard_map/all_gather | solution.py:81
  52.9 3.7 fusion.54
  56.6 59.7 %all-reduce.6.cloned.1.call-done = bf16[128,768]{1,0:T(8,128)(2,1)} async-done(((bf16[128,768]{1,0:T(8,128)(2,1)}), bf16[128,768]{1,0:T(8,128)(2,1)}) %all-reduce.6.cloned.1.call-update) | async-done | bytes 196624
  117.3 75.3 %reduce-scatter.3.cloned.1.call-done = bf16[16,384]{1,0:T(8,128)(2,1)} async-done(((bf16[512,384]{1,0:T(8,128)(2,1)}), bf16[16,384]{1,0:T(8,128)(2,1)}) %reduce-scatter.3.cloned.1.call-update) | async-done | bytes 12304 | tf_op jit(solution)/shard_map/reduce_scatter | solution.py:69
  193.3 26.6 %all_gather.13 = bf16[512,384]{1,0:T(8,128)(2,1)S(1)} all-gather(bf16[16,384]{1,0:T(8,128)(2,1)S(1)} %copy_bitcast_fusion.3), channel_id=1, replica_groups=mesh['cam'=32,'trk'=4] {'cam'}, dimensions={0}, use_global_device_ids=true | all-gather | bytes 405504 | tf_op jit(solution)/shard_map/all_gather | solution.py:73
  220.1 8.8 %fusion.23 = f32[24,1,768]{2,1,0:T(1,128)S(1)} fusion(bf16[24,768,384]{2,1,0:T(8,128)(2,1)} %param.16, bf16[24,384,1]{1,0,2:T(8,128)(2,1)S(1)} %fusion.2), kind=kOutput, calls=%fused_computation.43 | convolution fusion | flops 14155776 | bytes 14247936 | tf_op jit(solution)/shard_map/tq,tkq->tk/dot_general | solution.py:77
  229.2 13.1 %psum.43 = f32[4,768]{1,0:T(4,128)S(1)} all-reduce(f32[4,768]{1,0:T(4,128)S(1)} %convolution_subtract_fusion.1), channel_id=1, replica_groups=mesh['cam'=32,'trk'=4] {'trk'}, use_global_device_ids=true, to_apply=%region_5.0 | all-reduce | flops 3072 | bytes 24576 | tf_op jit(solution)/shard_map/psum | solution.py:95
  242.9 66.6 %all-reduce.2 = (f32[]{:T(128)}, f32[]{:T(128)}) all-reduce(f32[]{:T(128)} %get-tuple-element.3, f32[]{:T(128)} %get-tuple-element.2), channel_id=1, replica_groups=mesh['cam'=32,'trk'=4] {'cam'}, use_global_device_ids=true, to_apply=%region_1.0 | all-reduce | flops 2 | bytes 16 | tf_op jit(solution)/shard_map/psum | solution.py:53
  311.5 63.3 %psum.45 = f32[]{:T(128)} all-reduce(f32[]{:T(128)} %get-tuple-element.8), channel_id=1, replica_groups=mesh['cam'=32,'trk'=4] {'cam'}, use_global_device_ids=true, to_apply=%region_9.0 | all-reduce | flops 1 | bytes 8 | tf_op jit(solution)/shard_map/psum | solution.py:53
  376.5 3.1 fusion.45
  380.9 7.0 %fusion.13 = f32[24,1,384]{2,1,0:T(1,128)S(1)} fusion(bf16[24,768,384]{2,1,0:T(8,128)(2,1)} %param.16, bf16[24,768,1]{1,0,2:T(8,128)(2,1)S(1)} %fusion.1), kind=kOutput, calls=%fused_computation.30 | convolution fusion | flops 14155776 | bytes 14229504 | tf_op jit(solution)/shard_map/tk,tkq->tq/dot_general | solution.py:65
  387.9 1.7 convolution_convert_fusion
  389.6 22.2 %all-gather.1 = bf16[32,4,768]{2,1,0:T(4,128)(2,1)S(1)} all-gather(bf16[1,4,768]{2,1,0:T(4,128)(2,1)S(1)} %get-tuple-element.6), channel_id=1, replica_groups=mesh['cam'=32,'trk'=4] {'cam'}, dimensions={0}, use_global_device_ids=true | all-gather | bytes 202752 | tf_op jit(solution)/shard_map/all_gather | solution.py:81
  412.0 3.7 fusion.48
  415.7 58.3 %all-reduce.8.cloned.1.call-done = bf16[128,768]{1,0:T(8,128)(2,1)} async-done(((bf16[128,768]{1,0:T(8,128)(2,1)}), bf16[128,768]{1,0:T(8,128)(2,1)}) %all-reduce.8.cloned.1.call-update) | async-done | bytes 196624
  475.0 75.0 %reduce-scatter.5.cloned.1.call-done = bf16[16,384]{1,0:T(8,128)(2,1)} async-done(((bf16[512,384]{1,0:T(8,128)(2,1)}), bf16[16,384]{1,0:T(8,128)(2,1)}) %reduce-scatter.5.cloned.1.call-update) | async-done | bytes 12304 | tf_op jit(solution)/shard_map/reduce_scatter | solution.py:69
  550.8 26.3 %all_gather.15 = bf16[512,384]{1,0:T(8,128)(2,1)S(1)} all-gather(bf16[16,384]{1,0:T(8,128)(2,1)S(1)} %copy_bitcast_fusion.2), channel_id=1, replica_groups=mesh['cam'=32,'trk'=4] {'cam'}, dimensions={0}, use_global_device_ids=true | all-gather | bytes 405504 | tf_op jit(solution)/shard_map/all_gather | solution.py:73
  577.3 8.8 %fusion.20 = f32[24,1,768]{2,1,0:T(1,128)S(1)} fusion(bf16[24,768,384]{2,1,0:T(8,128)(2,1)} %param.16, bf16[24,384,1]{1,0,2:T(8,128)(2,1)S(1)} %fusion.3), kind=kOutput, calls=%fused_computation.40 | convolution fusion | flops 14155776 | bytes 14247936 | tf_op jit(solution)/shard_map/tq,tkq->tk/dot_general | solution.py:77
  586.4 13.1 %psum.46 = f32[4,768]{1,0:T(4,128)S(1)} all-reduce(f32[4,768]{1,0:T(4,128)S(1)} %convolution_subtract_fusion), channel_id=1, replica_groups=mesh['cam'=32,'trk'=4] {'trk'}, use_global_device_ids=true, to_apply=%region_13.0 | all-reduce | flops 3072 | bytes 24576 | tf_op jit(solution)/shard_map/psum | solution.py:95
  600.0 66.6 %psum.47 = f32[]{:T(128)} all-reduce(f32[]{:T(128)} %multiply_reduce_fusion.2), channel_id=1, replica_groups=mesh['cam'=32,'trk'=4] {'cam'}, use_global_device_ids=true, to_apply=%region_15.0 | all-reduce | flops 1 | bytes 8 | tf_op jit(solution)/shard_map/psum | solution.py:97
  (58 shorter events, 12.4 us)
Async XLA Ops:
  7.2 44.3 %copy-start.4 = (s32[4]{0:T(128)S(1)}, s32[4]{0:T(128)}, u32[]{:S(2)}) copy-start(s32[4]{0:T(128)} %param.23) | copy-start | bytes 52
  7.2 15.1 %copy-start.5 = (s32[24]{0:T(128)S(1)}, s32[24]{0:T(128)}, u32[]{:S(2)}) copy-start(s32[24]{0:T(128)} %param.19) | copy-start | bytes 292
  7.2 15.1 %copy-start.6 = (s32[24]{0:T(128)S(1)}, s32[24]{0:T(128)}, u32[]{:S(2)}) copy-start(s32[24]{0:T(128)} %param.18) | copy-start | bytes 292
  7.2 109.1 %all-reduce.6.cloned.1.call-start = ((), (), s32[]{:S(2)}) async-start(), calls=%async_computation.4 | async-start | bytes 393216
  8.8 42.8 %copy-start.9 = (u32[128]{0:T(128)S(1)}, u32[128]{0:T(128)}, u32[]{:S(2)}) copy-start(u32[128]{0:T(128)} %constant.20) | copy-start | bytes 1540
  11.9 104.4 %copy-start.7 = (s32[4]{0:T(128)S(1)}, s32[4]{0:T(128)}, u32[]{:S(2)}) copy-start(s32[4]{0:T(128)} %param.22) | copy-start | bytes 52
  11.9 181.4 %copy-start = (f32[16,9,128]{2,0,1:T(8,128)S(1)}, f32[16,9,128]{2,0,1:T(8,128)}, u32[]{:S(2)}) copy-start(f32[16,9,128]{2,0,1:T(8,128)} %param.15) | copy-start | bytes 221188
  13.7 178.9 %reduce-scatter.3.cloned.1.call-start = ((), (), s32[]{:S(2)}) async-start(), calls=%async_computation.2 | async-start | bytes 405504 | tf_op jit(solution)/shard_map/reduce_scatter | solution.py:69
  22.2 206.6 %copy-start.8 = (s32[24]{0:T(128)S(1)}, s32[24]{0:T(128)}, u32[]{:S(2)}) copy-start(s32[24]{0:T(128)} %param.17) | copy-start | bytes 292
  22.3 220.0 %copy-start.1 = (f32[4,768]{1,0:T(4,128)S(1)}, f32[4,768]{1,0:T(4,128)}, u32[]{:S(2)}) copy-start(f32[4,768]{1,0:T(4,128)} %param.13) | copy-start | bytes 36868
  22.3 220.0 %copy-start.2 = (f32[4,768]{1,0:T(4,128)S(1)}, f32[4,768]{1,0:T(4,128)}, u32[]{:S(2)}) copy-start(f32[4,768]{1,0:T(4,128)} %param.12) | copy-start | bytes 36868
  22.3 288.5 %copy-start.3 = (f32[4,768]{1,0:T(4,128)S(1)}, f32[4,768]{1,0:T(4,128)}, u32[]{:S(2)}) copy-start(f32[4,768]{1,0:T(4,128)} %param.14) | copy-start | bytes 36868
  24.0 450.0 %all-reduce.8.cloned.1.call-start = ((), (), s32[]{:S(2)}) async-start(), calls=%async_computation.5 | async-start | bytes 393216
  380.7 169.3 %reduce-scatter.5.cloned.1.call-start = ((), (), s32[]{:S(2)}) async-start(), calls=%async_computation.3 | async-start | bytes 405504 | tf_op jit(solution)/shard_map/reduce_scatter | solution.py:69
Sparse Core Ops, SparseCore 0:
  13.8 102.3 all-reduce.5
  120.1 72.3 reduce-scatter.2
  380.8 93.1 all-reduce.7
  477.3 72.6 reduce-scatter.4
where the time goes:
time: 676 us; the launch traced here: 675 us
  blocking collectives  325 us (48%)
  waiting for transfers between devices  268 us (40%)
  matrix products  56.6 us (8%)
  between operations  19.3 us (3%)
    reduce_scatter x2, waiting for transfers between devices, shards(): lax.psum_scatter(dense_sums.astype(jnp.bfloat16), 'cam', scatter_dimensio...  150 us
    psum x2, blocking collectives, scaled_inner(): return lax.psum(jnp.sum(residual * scaled), 'cam')  130 us
    unnamed x6, waiting for transfers between devices  118 us
    psum x1, blocking collectives, shards(): alpha = inner_now / lax.psum(jnp.sum(direction * image), 'cam')  66.6 us
    all_gather x2, blocking collectives, shards(): every_value = lax.all_gather(point_values, 'cam', axis=0, tiled=True)  52.9 us
    all_gather x2, blocking collectives, shards(): everyone = lax.all_gather(rounded, 'cam', axis=0, tiled=True)  49.6 us
    psum x2, blocking collectives, shards(): summed = lax.psum(coupled_rows + mirror_own - schur, 'trk')  26.2 us
    dot_general x2, matrix products, shards(): jnp.einsum('tq,tkq->tk', returned_vals, tiles, preferred_element_type=jnp...  17.5 us
  transfers between devices with their start and end apart: 4, of which 4 were waited for; matrix products, arithmetic and copies ran while one was open for 4% of the time, Pallas kernels for 0%

commit v1 on v0

v1 whole, which is shorter than its diff:
```python
import jax
import jax.numpy as jnp
from jax import lax
from jax.experimental import pallas as pl
from jax.experimental.pallas import tpu as pltpu
from jax.sharding import PartitionSpec as P

MESH = pl.DeviceIdType.MESH
F32, BF16, I32 = jnp.float32, jnp.bfloat16, jnp.int32
CAMS = 32
TRKS = 4
TILES = 24
PAIRS = 4
KB = 768
TQ = 384
NN = (((1,), (0,)), ((), ()))
NT = (((1,), (1,)), ((), ()))


def iota(shape, dim):
    return lax.broadcasted_iota(I32, shape, dim)


def hot(mask):
    return jnp.where(mask, 1.0, 0.0).astype(BF16)


def dot(a, b, dims=NN):
    return lax.dot_general(a, b, dims, preferred_element_type=F32)


def total(a):
    return jnp.sum(jnp.sum(a, axis=0, keepdims=True), axis=1, keepdims=True)


def pack(dup):
    low = iota((8, 128), 0) < 4
    return jnp.concatenate(
        [jnp.where(low, dup[:, 256 * j : 256 * j + 128], dup[:, 256 * j + 128 : 256 * j + 256]) for j in range(3)],
        axis=0,
    )


def unpack(packed):
    low = iota((8, 128), 0) < 4
    parts = []
    for j in range(3):
        here = packed[8 * j : 8 * j + 8]
        turned = pltpu.roll(here, 4, 0)
        parts += [jnp.where(low, here, turned), jnp.where(low, turned, here)]
    return jnp.concatenate(parts, axis=1)


def triple(row):
    high = row.astype(BF16).astype(F32)
    rest = row - high
    mid = rest.astype(BF16).astype(F32)
    low = rest - mid
    sub = iota((8, 128), 0)
    return jnp.where(sub == 0, high, jnp.where(sub == 1, mid, jnp.where(sub == 2, low, 0.0)))


def peer_of(me, j):
    def hop(k):
        return jnp.where(k == 2, 3, jnp.where(k == 3, 0, 2 - k))

    z, x, core = me // 8, (me // 2) % 4, me % 2
    return ((z + hop(j // 8)) % 4) * 8 + ((x + hop((j // 2) % 4)) % 4) * 2 + (core + 1 - j % 2) % 2


def kernel(
    grad_ref, diag_ref, prec_ref, inv_ref, tiles_hbm, blk_ref, own_ref, trk_ref, live_ref, covis_hbm, prow_ref, pcol_ref,
    step_ref, res_ref,
    tiles, covis, wide, stack, send_vec, recv_vec, send_mir, recv_mir, send_sum, recv_sum, send_val, recv_val,
    send_tot, recv_tot, to_slots, from_slots, gather_rows, scatter_rows, pick_cols, add_mir,
    tile_sem, covis_sem, send_sem, recv_sem,
):
    me, trk = lax.axis_index("cam"), lax.axis_index("trk")

    def load_tile(i):
        return pltpu.make_async_copy(tiles_hbm.at[i], tiles.at[i], tile_sem.at[i])

    def load_pair(k):
        return pltpu.make_async_copy(covis_hbm.at[k], covis.at[k], covis_sem.at[k])

    barrier = pltpu.get_barrier_semaphore()

    def greet(j, carry):
        pl.semaphore_signal(barrier, inc=1, device_id=(peer_of(me, j), trk), device_id_type=MESH)
        return carry

    lax.fori_loop(0, CAMS - 1, greet, 0)
    for j in range(1, TRKS):
        pl.semaphore_signal(barrier, inc=1, device_id=(me, (trk + j) % TRKS), device_id_type=MESH)

    def start_tile(i, carry):
        load_tile(i).start()
        return carry

    lax.fori_loop(0, TILES, start_tile, 0)
    for k in range(PAIRS):
        load_pair(k).start()

    def send_all(src, dst, rows, sem, own_part):
        def step(j, carry):
            peer = peer_of(me, j)
            part = src.at[pl.ds(pl.multiple_of(peer * rows, rows), rows)] if own_part else src
            pltpu.make_async_remote_copy(
                part,
                dst.at[pl.ds(pl.multiple_of(me * rows, rows), rows)],
                send_sem.at[sem],
                recv_sem.at[sem],
                device_id=(peer, trk),
                device_id_type=MESH,
            ).start()
            return carry

        lax.fori_loop(0, CAMS - 1, step, 0)

    def wait_all(dst, rows, sem, sems):
        part = dst.at[pl.ds(0, (CAMS - 1) * rows)]
        pltpu.make_async_copy(part, part, sems.at[sem]).wait()

    def mine(rows):
        return pl.ds(pl.multiple_of(me * rows, rows), rows)

    def doubled(ref):
        value = ref[...]
        return jnp.concatenate([value, value], axis=0)

    grad, diag, prec = doubled(grad_ref), doubled(diag_ref), doubled(prec_ref)
    first = prec * grad

    lane = iota((1, 128), 1)
    lane32 = lane & 31
    eye = iota((128, 128), 0) == iota((128, 128), 1)

    def to_col(row):
        return jnp.sum(jnp.where(eye, row, 0.0), axis=1, keepdims=True)

    owner = jnp.full((1, 128), -1, I32)
    track = jnp.zeros((1, 128), I32)
    block = jnp.full((1, 128), -1, I32)
    for i in range(TILES):
        here = lane32 == i
        owner = jnp.where(here, own_ref[i], owner)
        track = jnp.where(here, trk_ref[i], track)
        block = jnp.where(here, blk_ref[i], block)
    owner = jnp.where(lane32 < live_ref[0], owner, -1).astype(F32)
    owner_col = to_col(owner)
    track_col = to_col(track.astype(F32))
    block_col = to_col(block.astype(F32))
    earlier = (owner_col[:32] == owner) & (iota((32, 128), 0) < lane32) & (owner >= 0.0)
    rank = jnp.sum(jnp.where(earlier, 1.0, 0.0), axis=0, keepdims=True)
    rank_col = to_col(rank)
    slot = jnp.where(
        (owner >= 0.0) & (lane < 96), owner * 16.0 + (lane >> 5).astype(F32) * 4.0 + rank, -1.0
    )
    slot_col = to_col(slot)
    slot_of = jnp.where(owner_col >= 0.0, owner_col * 4.0 + rank_col, -1.0)[:32]
    table = jnp.sum(
        jnp.where(slot_of == iota((32, 128), 1).astype(F32), track_col[:32] + 1.0, 0.0), axis=0, keepdims=True
    )
    pair_cols = jnp.zeros((1, 128), I32)
    for k in range(PAIRS):
        pair_cols = jnp.where((lane & 3) == k, pcol_ref[k], pair_cols)
    sub8 = iota((8, 128), 0)
    routes = jnp.where(sub8 == 0, table, jnp.where(sub8 == 1, pair_cols.astype(F32), 0.0))

    def pack_send(vec, extra, send, recv, sem):
        message = jnp.concatenate([pack(vec), extra], axis=0).astype(BF16)
        send[...] = message
        recv[mine(32), :] = message
        send_all(send, recv, 32, sem, False)

    pl.semaphore_wait(barrier, CAMS - 1 + TRKS - 1)
    pack_send(first, routes, send_vec.at[0], recv_vec.at[0], 0)

    to_slots[...] = hot(iota((512, 128), 0).astype(F32) == slot)
    extra_rows = iota((128, 512), 0) - 96
    from_slots[...] = hot(
        (iota((128, 512), 1).astype(F32) == slot_col)
        | ((extra_rows >= 0) & (extra_rows < 3) & ((iota((128, 512), 1) & 15) == 12 + extra_rows))
    )
    row64 = iota((64, 1), 0)
    base = jnp.zeros((64, 1), I32)
    for k in range(PAIRS):
        base = jnp.where((row64 & 3) == k, (pcol_ref[k] // 4) * 32 + pcol_ref[k] % 4, base)
    base = base + (row64 >> 3) * 4
    wide_lane = iota((64, 1024), 1)
    pick_cols[...] = hot(
        ((row64 < 48) & (wide_lane == base)) | ((row64 >= 48) & (row64 < 56) & ((wide_lane & 31) == row64 - 24))
    )
    stack[...] = jnp.zeros((128, 128), F32)
    rows8 = iota((8, 1), 0)
    prow_col = jnp.zeros((8, 1), I32)
    for k in range(PAIRS):
        prow_col = jnp.where((rows8 & 3) == k, prow_ref[k], prow_col)
    rows_wide = iota((8, KB), 0)
    rows_tq = iota((8, TQ), 0)

    def unstack(rows, at, count):
        return jnp.concatenate([rows[at * j : at * j + 8] for j in range(count)], axis=1)

    def forward(vec, load):
        picked = jnp.zeros((32, KB), F32)
        for b in range(4):
            picked = jnp.where(block_col[:32] == b, vec[b : b + 1], picked)
        wide[...] = picked

        def group(g, carry):
            here = wide[pl.ds(pl.multiple_of(g * 8, 8), 8), :]
            out = jnp.zeros((8, TQ), F32)
            for r in range(8):
                if load:
                    load_tile(g * 8 + r).wait()
                out = out + dot(jnp.where(rows_wide == r, here, 0.0).astype(BF16), tiles[g * 8 + r])
            for j in range(3):
                stack[pl.ds(pl.multiple_of(j * 32 + g * 8, 8), 8), :] = out[:, 128 * j : 128 * j + 128]
            return carry

        lax.fori_loop(0, TILES // 8, group, 0)

    def couple(vec):
        rows = jnp.zeros((8, KB), F32)
        for b in range(4):
            rows = jnp.where(prow_col == b, vec[b : b + 1], rows)
        mirrored = jnp.zeros((8, KB), F32)
        for k in range(PAIRS):
            mirrored = mirrored + dot(jnp.where((rows_wide & 3) == k, rows, 0.0).astype(BF16), covis[k])
        return mirrored

    def couple_rows(cols):
        out = jnp.zeros((8, KB), F32)
        for k in range(PAIRS):
            lhs = jnp.where((rows_wide & 3) == prow_ref[k], cols[k : k + 1], 0.0).astype(BF16)
            out = out + dot(lhs, covis[k], NT)
        return out

    def backward(values, start):
        out = start
        for g in range(TILES // 8):
            here = jnp.concatenate([values[32 * j + 8 * g : 32 * j + 8 * g + 8] for j in range(3)], axis=1)
            for r in range(8):
                lhs = jnp.where((rows_tq & 3) == blk_ref[g * 8 + r], here[r : r + 1], 0.0).astype(BF16)
                out = out - dot(lhs, tiles[g * 8 + r], NT)
        return out

    def points(sums):
        parts = []
        for a in range(3):
            part = jnp.zeros((16, 128), F32)
            for e in range(3):
                part = part + inv_ref[3 * a + e] * sums[16 * e : 16 * e + 16]
            parts.append(part)
        return jnp.concatenate(parts, axis=0)

    forward(first, True)
    send_sum[0] = dot(to_slots[...], stack[...].astype(BF16)).astype(BF16)
    recv_sum[0, mine(16), :] = send_sum[0, mine(16), :]
    send_all(send_sum.at[0], recv_sum.at[0], 16, 1, True)

    wait_all(recv_vec.at[0], 32, 0, recv_sem)
    got = recv_vec[0]
    cols = unstack(dot(pick_cols[...], got), 8, 6)
    select = iota((64, 1024), 0)
    source = iota((64, 1024), 1)
    tables = dot(hot(source == (select & 31) * 32 + 24 + (select >> 5)), got)
    mine4 = dot(tables[:32].astype(BF16), hot(iota((128, 128), 0) == me * 4 + (iota((128, 128), 1) & 3)))
    row_codes, col_codes = [], []
    sub32, lane32x = iota((32, 128), 0), iota((32, 128), 1)
    chunk = (lane >> 2) & 3
    for q in range(4):
        value = jnp.sum(jnp.where(sub32 == 8 * q + (lane32x >> 4), mine4, 0.0), axis=0, keepdims=True)
        code = jnp.where((value > 0.0) & (chunk < 3), chunk.astype(F32) * 16.0 + value - 1.0, -1.0)
        row_codes.append(code)
        code = jnp.where((chunk == 3) & ((lane & 3) < 3), 48.0 + (lane & 3).astype(F32), code)
        col_codes.append(to_col(code))
    gather_rows[...] = hot(iota((48, 512), 0).astype(F32) == jnp.concatenate(row_codes, axis=1))
    scatter_rows[...] = hot(iota((512, 128), 1).astype(F32) == jnp.concatenate(col_codes, axis=0))
    mir_codes = []
    part = (lane >> 2) & 7
    for q in range(8):
        value = jnp.sum(jnp.where(sub32 == 4 * q + (lane32x >> 5), tables[32:], 0.0), axis=0, keepdims=True)
        local = value - (me * 4).astype(F32)
        code = jnp.where((local >= 0.0) & (local < 4.0), part.astype(F32) * 4.0 + local, -1.0)
        mir_codes.append(jnp.where(part < 6, code, (lane & 31).astype(F32)))
    add_mir[...] = hot(iota((32, 1024), 0).astype(F32) == jnp.concatenate(mir_codes, axis=1))

    for k in range(PAIRS):
        load_pair(k).wait()
    mirrored = couple(first)
    pack_send(mirrored, jnp.zeros((8, 128), F32), send_mir.at[0], recv_mir.at[0], 2)

    def owners(sums_recv, vals_send, vals_recv, sem, extra):
        sums = dot(gather_rows[...], sums_recv[...])
        values = points(sums)
        fill = jnp.concatenate([values, extra(sums, values), jnp.zeros((72, 128), F32)], axis=0).astype(BF16)
        vals_send[...] = dot(scatter_rows[...], fill).astype(BF16)
        vals_recv[mine(16), :] = vals_send[mine(16), :]
        send_all(vals_send, vals_recv, 16, sem, True)

    wait_all(recv_sum.at[0], 16, 1, recv_sem)
    quad = total(cols * mirrored) + 0.125 * total(first * diag * first)
    owned_inner = 0.125 * total(grad * first)
    owners(
        recv_sum.at[0],
        send_val.at[0],
        recv_val.at[0],
        3,
        lambda s, v: triple(jnp.where(lane == 0, quad - total(s * v), jnp.where(lane == 1, owned_inner, 0.0))),
    )
    coupled = couple_rows(cols)

    def exchange(message, send, recv, sem):
        send[...] = message
        for j in range(1, TRKS):
            pltpu.make_async_remote_copy(
                send,
                recv.at[trk],
                send_sem.at[sem],
                recv_sem.at[sem],
                device_id=(me, (trk + j) % TRKS),
                device_id_type=MESH,
            ).start()
        recv[trk] = message
        part = recv.at[pl.ds(0, TRKS - 1)]
        pltpu.make_async_copy(part, part, recv_sem.at[sem]).wait()
        return (recv[0] + recv[1]) + (recv[2] + recv[3])

    wait_all(recv_mir.at[0], 32, 2, recv_sem)
    mir = dot(add_mir[...], recv_mir[0])
    wait_all(recv_val.at[0], 16, 3, recv_sem)
    values = dot(from_slots[...], recv_val[0])
    quads = values[96:97] + values[97:98] + values[98:99]
    local = backward(values, coupled)
    message = jnp.concatenate([pack(local) + mir[:24], jnp.where(sub8 == 0, quads, 0.0)], axis=0)
    summed = exchange(message, send_tot.at[0], recv_tot.at[0], 4)
    image = diag * first + unpack(summed[:24])

    dim, rz = summed[24:25, 0:1], summed[24:25, 1:2]
    alpha = rz / dim
    residual = grad - alpha * image

    vec = prec * residual
    inner = jnp.where(lane == 0, 0.5 * total(residual * vec), jnp.where(lane == 1, 0.5 * total(vec * image), 0.0))
    pack_send(vec, triple(inner), send_vec.at[1], recv_vec.at[1], 5)
    forward(vec, False)
    send_sum[1] = dot(to_slots[...], stack[...].astype(BF16)).astype(BF16)
    recv_sum[1, mine(16), :] = send_sum[1, mine(16), :]
    send_all(send_sum.at[1], recv_sum.at[1], 16, 6, True)

    wait_all(recv_vec.at[1], 32, 5, recv_sem)
    got = dot(pick_cols[...], recv_vec[1])
    cols = unstack(got, 8, 6)
    inners = got[48:49] + got[49:50] + got[50:51]
    fresh, cross = inners[:, 0:1], inners[:, 1:2]
    beta = fresh / rz
    direction = vec + beta * first
    mirrored = couple(vec)
    pack_send(mirrored, jnp.zeros((8, 128), F32), send_mir.at[1], recv_mir.at[1], 7)
    quad = total(cols * mirrored) + 0.125 * total(vec * diag * vec)

    wait_all(recv_sum.at[1], 16, 6, recv_sem)
    owners(
        recv_sum.at[1],
        send_val.at[1],
        recv_val.at[1],
        8,
        lambda s, v: triple(jnp.where(lane == 0, quad - total(s * v), 0.0)),
    )
    coupled = couple_rows(cols)
    wait_all(recv_mir.at[1], 32, 7, recv_sem)
    mir = dot(add_mir[...], recv_mir[1])
    wait_all(recv_val.at[1], 16, 8, recv_sem)
    values = dot(from_slots[...], recv_val[1])
    quads = values[96:97] + values[97:98] + values[98:99]
    local = backward(values, coupled)
    message = jnp.concatenate(
        [pack(local) + mir[:24], jnp.where(sub8 == 0, quads, 0.0)], axis=0
    )
    summed = exchange(message, send_tot.at[1], recv_tot.at[1], 9)
    second = diag * vec + unpack(summed[:24]) + beta * image
    curve = summed[24:25, 0:1] + beta * (2.0 * cross + beta * dim)
    alpha_next = fresh / curve
    step_ref[...] = (alpha * first + alpha_next * direction)[:4]
    res_ref[...] = (residual - alpha_next * second)[:4]

    for it in range(2):
        wait_all(recv_vec.at[it], 32, 5 * it, send_sem)
        wait_all(recv_sum.at[it], 16, 5 * it + 1, send_sem)
        wait_all(recv_mir.at[it], 32, 5 * it + 2, send_sem)
        wait_all(recv_val.at[it], 16, 5 * it + 3, send_sem)
        part = recv_tot.at[it, pl.ds(0, TRKS - 1)]
        pltpu.make_async_copy(part, part, send_sem.at[5 * it + 4]).wait()


def shards(*args):
    args = args[:3] + (jnp.transpose(args[3], (1, 0, 2)),) + args[4:]
    vmem = pl.BlockSpec(memory_space=pltpu.VMEM)
    smem = pl.BlockSpec(memory_space=pltpu.SMEM)
    hbm = pl.BlockSpec(memory_space=pl.ANY)
    out = jax.ShapeDtypeStruct((4, KB), F32)
    return pl.pallas_call(
        kernel,
        out_shape=(out, out),
        in_specs=[vmem, vmem, vmem, vmem, hbm, smem, smem, smem, smem, hbm, smem, smem],
        out_specs=(vmem, vmem),
        scratch_shapes=[
            pltpu.VMEM((TILES, KB, TQ), BF16),
            pltpu.VMEM((PAIRS, KB, KB), BF16),
            pltpu.VMEM((32, KB), F32),
            pltpu.VMEM((128, 128), F32),
            pltpu.VMEM((2, 32, 128), BF16),
            pltpu.VMEM((2, 1024, 128), BF16),
            pltpu.VMEM((2, 32, 128), BF16),
            pltpu.VMEM((2, 1024, 128), BF16),
            pltpu.VMEM((2, 512, 128), BF16),
            pltpu.VMEM((2, 512, 128), BF16),
            pltpu.VMEM((2, 512, 128), BF16),
            pltpu.VMEM((2, 512, 128), BF16),
            pltpu.VMEM((2, 32, 128), F32),
            pltpu.VMEM((2, TRKS, 32, 128), F32),
            pltpu.VMEM((512, 128), BF16),
            pltpu.VMEM((128, 512), BF16),
            pltpu.VMEM((48, 512), BF16),
            pltpu.VMEM((512, 128), BF16),
            pltpu.VMEM((64, 1024), BF16),
            pltpu.VMEM((32, 1024), BF16),
            pltpu.SemaphoreType.DMA((TILES,)),
            pltpu.SemaphoreType.DMA((PAIRS,)),
            pltpu.SemaphoreType.DMA((10,)),
            pltpu.SemaphoreType.DMA((10,)),
        ],
        compiler_params=pltpu.CompilerParams(
            collective_id=1, has_side_effects=True, vmem_limit_bytes=56 * 2**20
        ),
        cost_estimate=pl.CostEstimate(flops=8 * 2 * 2 * 9_400_000, bytes_accessed=19_000_000, transcendentals=0),
        name="cg",
    )(*args)


def solution(mesh):
    vec, both = P("cam", None), ("cam", "trk")
    tile, line = P(both, None, None), P(both)
    in_specs = (vec, vec, vec, tile, tile, line, line, line, line, tile, line, line)
    return jax.shard_map(shards, mesh=mesh, in_specs=in_specs, out_specs=(vec, vec), check_vma=False)
```

time: 676 us -> 59.7 us (0.09)
  blocking collectives: 325 us -> 0 us
  waiting for transfers between devices: 268 us -> 0 us
  matrix products: 56.6 us -> 0 us
  Pallas kernels: 0 us -> 55.5 us
  between operations: 19.3 us -> 1.29 us
    psum x5 -> x0, blocking collectives: 223 us -> none  [the longest x2 130 us: scaled_inner(): return lax.psum(jnp.sum(residual * scaled), 'cam')]
    reduce_scatter x2 -> x0, waiting for transfers between devices: 150 us -> none  [shards(): lax.psum_scatter(dense_sums.astype(jnp.bfloat16), 'cam', scatter_dimensio...]
    unnamed x6 -> x0, waiting for transfers between devices: 118 us -> none
    all_gather x4 -> x0, blocking collectives: 102 us -> none  [the longest x2 52.9 us: shards(): every_value = lax.all_gather(point_values, 'cam', axis=0, tiled=True)]
    dot_general x24 -> x0, matrix products: 56.6 us -> none  [the longest x2 17.5 us: shards(): jnp.einsum('tq,tkq->tk', returned_vals, tiles, preferred_element_type=jnp...]
    pallas_call x0 -> x1, Pallas kernels: none -> 55.5 us  [shards(): pl.pallas_call(kernel, out_shape=(out, out), in_specs=[vmem, vmem, vmem,...]
  transfers between devices with their start and end apart: 4 -> 0, of which waited for: 4 -> 0; matrix products, arithmetic and copies ran while one was open for 4% -> 0% of each run, Pallas kernels for 0% -> 0%
where the time goes in v1:
time: 59.7 us; the launch traced here: 59.4 us
  Pallas kernels  55.5 us (93%)
  local copies, waits for them, and re-layouts  2.61 us (4%)
  between operations  1.29 us (2%)
    pallas_call x1, Pallas kernels, shards(): pl.pallas_call(kernel, out_shape=(out, out), in_specs=[vmem, vmem, vmem,...  55.5 us
    unnamed x2, local copies, waits for them, and re-layouts  2.61 us

profile of v1, /device:TPU:1, one launch (start us, length us, event | category | flops | bytes accessed | tf_op | source)
XLA Modules:
  0.0 59.4 jit_solution(12101311982426718607)
XLA Ops:
  1.3 55.5 %cg.1 = (f32[4,768]{1,0:T(4,128)}, f32[4,768]{1,0:T(4,128)}) custom-call(f32[4,768]{1,0:T(4,128)} %grad_ref.1, f32[4,768]{1,0:T(4,128)} %diag_ref.1, f32[4,768]{1,0:T(4,128)} %prec_ref.1, f32[9,16,128]{2,1,0:T(8,128)} %bitcast.1, bf16[24,768,384]{2,1,0:T(8,128)(2,1)} %tiles_hbm.1, s32[24]{0:T(128)} %blk_ref.1, s32[24]{0:T(128)} %own_ref.1, s32[24]{0:T(128)} %trk_ref.1, ...), custom_call_target="tpu_custom_call" | custom-call | flops 300800000 | bytes 19000000 | tf_op jit(solution)/shard_map/cg/pallas_call | solution.py:404
  56.8 1.3 %copy.17 = f32[4,768]{1,0:T(4,128)} copy(f32[4,768]{1,0:T(4,128)} %get-tuple-element.4) | data formatting | bytes 24576
  58.1 1.3 %copy.18 = f32[4,768]{1,0:T(4,128)} copy(f32[4,768]{1,0:T(4,128)} %get-tuple-element.5) | data formatting | bytes 24576

commit v2 on v1

v2 whole, which is shorter than its diff:
```python
import jax
import jax.numpy as jnp
from jax import lax
from jax.experimental import pallas as pl
from jax.experimental.pallas import tpu as pltpu
from jax.sharding import PartitionSpec as P

MESH = pl.DeviceIdType.MESH
F32, BF16, I32 = jnp.float32, jnp.bfloat16, jnp.int32
CAMS = 32
TRKS = 4
TILES = 24
PAIRS = 4
KB = 768
TQ = 384
CHUNK = 4
EARLY = 3
NN = (((1,), (0,)), ((), ()))
NT = (((1,), (1,)), ((), ()))


def iota(shape, dim):
    return lax.broadcasted_iota(I32, shape, dim)


def hot(mask):
    return jnp.where(mask, 1.0, 0.0).astype(BF16)


def dot(a, b, dims=NN):
    return lax.dot_general(a, b, dims, preferred_element_type=F32)


def total(a):
    return jnp.sum(jnp.sum(a, axis=0, keepdims=True), axis=1, keepdims=True)


def pack(dup):
    low = iota((8, 128), 0) < 4
    return jnp.concatenate(
        [jnp.where(low, dup[:, 256 * j : 256 * j + 128], dup[:, 256 * j + 128 : 256 * j + 256]) for j in range(3)],
        axis=0,
    )


def unpack(packed):
    low = iota((8, 128), 0) < 4
    parts = []
    for j in range(3):
        here = packed[8 * j : 8 * j + 8]
        turned = pltpu.roll(here, 4, 0)
        parts += [jnp.where(low, here, turned), jnp.where(low, turned, here)]
    return jnp.concatenate(parts, axis=1)


def triple(row):
    high = row.astype(BF16).astype(F32)
    rest = row - high
    mid = rest.astype(BF16).astype(F32)
    low = rest - mid
    sub = iota((8, 128), 0)
    return jnp.where(sub == 0, high, jnp.where(sub == 1, mid, jnp.where(sub == 2, low, 0.0)))


def kernel(
    grad_hbm, diag_hbm, prec_hbm, inv_hbm, tiles_hbm, blk_hbm, own_hbm, trk_hbm, live_hbm, covis_hbm, prow_hbm, pcol_hbm,
    both_ref,
    tiles, flipped, covis, grad_ref, diag_ref, prec_ref, inv_ref, blk_ref, own_ref, trk_ref, live_ref, prow_ref, pcol_ref,
    wide, stack, send_vec, recv_vec, send_mir, recv_mir, send_sum, recv_sum, send_val, recv_val,
    send_tot, recv_tot, to_slots, from_slots, gather_rows, scatter_rows, pick_cols, add_mir,
    load_sem, tile_sem, covis_sem, send_sem, recv_sem,
):
    me, trk = lax.axis_index("cam"), lax.axis_index("trk")
    core, chip = me % 2, me // 2

    small = [
        pltpu.make_async_copy(src, dst, load_sem.at[i])
        for i, (src, dst) in enumerate(
            (
                (own_hbm, own_ref),
                (trk_hbm, trk_ref),
                (blk_hbm, blk_ref),
                (live_hbm, live_ref),
                (prow_hbm, prow_ref),
                (pcol_hbm, pcol_ref),
                (grad_hbm, grad_ref),
                (diag_hbm, diag_ref),
                (prec_hbm, prec_ref),
                (inv_hbm, inv_ref),
            )
        )
    ]
    for copy in small:
        copy.start()

    def load_chunk(c):
        part = pl.ds(c * CHUNK, CHUNK)
        return pltpu.make_async_copy(tiles_hbm.at[part], tiles.at[part], tile_sem.at[c])

    load_pairs = pltpu.make_async_copy(covis_hbm, covis, covis_sem)
    for c in range(TILES // CHUNK):
        load_chunk(c).start()
    load_pairs.start()

    barrier = pltpu.get_barrier_semaphore()

    def far_first(j):
        m = 31 - j
        return m ^ ((m >> 1) & 10)

    def greet(j, carry):
        pl.semaphore_signal(barrier, inc=1, device_id=(me ^ far_first(j), trk), device_id_type=MESH)
        return carry

    lax.fori_loop(0, CAMS - 1, greet, 0)
    for j in range(1, TRKS):
        pl.semaphore_signal(barrier, inc=1, device_id=(me, trk ^ j), device_id_type=MESH)

    def remote(src, dst, sem, to):
        pltpu.make_async_remote_copy(
            src, dst, send_sem.at[sem], recv_sem.at[sem], device_id=to, device_id_type=MESH
        ).start()

    def wait_rows(ref, rows, sem):
        part = ref.at[pl.ds(0, rows)]
        pltpu.make_async_copy(part, part, sem).wait()

    def exchange_all(src, dst, sem):
        def step(j, carry):
            peer = me ^ far_first(j)
            part = src.at[pl.ds(pl.multiple_of(peer * 16, 16), 16)]
            remote(part, dst.at[pl.ds(pl.multiple_of(me * 16, 16), 16)], sem, (peer, trk))
            return carry

        lax.fori_loop(0, CAMS - 1, step, 0)

    mine = pl.ds(pl.multiple_of(me * 16, 16), 16)
    place = pl.ds(pl.multiple_of(core * 512 + chip * 32, 32), 32)
    half = pl.ds(pl.multiple_of(core * 512, 512), 512)

    def gather_start(message, src, dst, sem):
        src[...] = message
        dst[place, :] = message

        def step(j, carry):
            m = 15 - j
            m = m ^ ((m >> 1) & 5)
            remote(src, dst.at[place], sem, (me ^ (2 * m), trk))
            return carry

        lax.fori_loop(0, CAMS // 2 - 1, step, 0)

    def gather_relay(dst, sem):
        wait_rows(dst, 480, recv_sem.at[sem])
        remote(dst.at[half], dst.at[half], sem + 1, (me ^ 1, trk))

    def gather_end(dst, sem):
        wait_rows(dst, 512, recv_sem.at[sem + 1])

    for copy in small[:-1]:
        copy.wait()

    def doubled(ref):
        value = ref[...]
        return jnp.concatenate([value, value], axis=0)

    grad, diag, prec = doubled(grad_ref), doubled(diag_ref), doubled(prec_ref)
    first = prec * grad

    lane = iota((1, 128), 1)
    lane32 = lane & 31
    eye = iota((128, 128), 0) == iota((128, 128), 1)

    def to_col(row):
        return jnp.sum(jnp.where(eye, row, 0.0), axis=1, keepdims=True)

    owner = jnp.full((1, 128), -1, I32)
    track = jnp.zeros((1, 128), I32)
    block = jnp.full((1, 128), -1, I32)
    for i in range(TILES):
        here = lane32 == i
        owner = jnp.where(here, own_ref[i], owner)
        track = jnp.where(here, trk_ref[i], track)
        block = jnp.where(here, blk_ref[i], block)
    owner = jnp.where(lane32 < live_ref[0], owner, -1).astype(F32)
    owner_col = to_col(owner)
    track_col = to_col(track.astype(F32))
    block_col = to_col(block.astype(F32))
    earlier = (owner_col[:32] == owner) & (iota((32, 128), 0) < lane32) & (owner >= 0.0)
    rank = jnp.sum(jnp.where(earlier, 1.0, 0.0), axis=0, keepdims=True)
    rank_col = to_col(rank)
    slot = jnp.where(
        (owner >= 0.0) & (lane < 96), owner * 16.0 + (lane >> 5).astype(F32) * 4.0 + rank, -1.0
    )
    slot_col = to_col(slot)
    slot_of = jnp.where(owner_col >= 0.0, owner_col * 4.0 + rank_col, -1.0)[:32]
    table = jnp.sum(
        jnp.where(slot_of == iota((32, 128), 1).astype(F32), track_col[:32] + 1.0, 0.0), axis=0, keepdims=True
    )
    pair_cols = jnp.zeros((1, 128), I32)
    for k in range(PAIRS):
        pair_cols = jnp.where((lane & 3) == k, pcol_ref[k], pair_cols)
    sub8 = iota((8, 128), 0)
    routes = jnp.where(sub8 == 0, table, jnp.where(sub8 == 1, pair_cols.astype(F32), 0.0))

    def with_rows(packed, extra):
        return jnp.concatenate([packed, extra], axis=0)

    pl.semaphore_wait(barrier, CAMS - 1 + TRKS - 1)

    gather_start(with_rows(pack(first), routes).astype(BF16), send_vec.at[0], recv_vec.at[0], 0)

    to_slots[...] = hot(iota((512, 128), 0).astype(F32) == slot)
    extra_rows = iota((128, 512), 0) - 96
    from_slots[...] = hot(
        (iota((128, 512), 1).astype(F32) == slot_col)
        | ((extra_rows >= 0) & (extra_rows < 3) & ((iota((128, 512), 1) & 15) == 12 + extra_rows))
    )
    row48 = iota((48, 1), 0)
    base = jnp.zeros((48, 1), I32)
    for k in range(PAIRS):
        cam = pcol_ref[k] // 4
        base = jnp.where((row48 & 3) == k, (cam % 2) * 512 + (cam // 2) * 32 + pcol_ref[k] % 4, base)
    base = base + (row48 >> 3) * 4
    pick_cols[...] = hot(iota((48, 1024), 1) == base)
    stack[...] = jnp.zeros((128, 128), F32)
    rows8 = iota((8, 1), 0)
    prow_col = jnp.zeros((8, 1), I32)
    for k in range(PAIRS):
        prow_col = jnp.where((rows8 & 3) == k, prow_ref[k], prow_col)
    rows_wide = iota((8, KB), 0)
    rows_tq = iota((8, TQ), 0)

    def unstack(rows, at, count):
        return jnp.concatenate([rows[at * j : at * j + 8] for j in range(count)], axis=1)

    def forward(vec, load):
        picked = jnp.zeros((32, KB), F32)
        for b in range(4):
            picked = jnp.where(block_col[:32] == b, vec[b : b + 1], picked)
        wide[...] = picked

        def group(g, carry):
            here = wide[pl.ds(pl.multiple_of(g * 8, 8), 8), :]
            out = jnp.zeros((8, TQ), F32)
            for r in range(8):
                if load and r % CHUNK == 0:
                    load_chunk(g * (8 // CHUNK) + r // CHUNK).wait()
                out = out + dot(jnp.where(rows_wide == r, here, 0.0).astype(BF16), tiles[g * 8 + r])
                if load and r % CHUNK < EARLY:
                    flip(g * 8 + r)
            for j in range(3):
                stack[pl.ds(pl.multiple_of(j * 32 + g * 8, 8), 8), :] = out[:, 128 * j : 128 * j + 128]
            return carry

        lax.fori_loop(0, TILES // 8, group, 0)

    def send_sums(src, dst, sem):
        src[...] = dot(to_slots[...], stack[...].astype(BF16)).astype(BF16)
        dst[mine, :] = src[mine, :]
        exchange_all(src, dst, sem)

    def flip(i):
        flipped[i] = tiles[i].T

    def flip_late(c, carry):
        for r in range(EARLY, CHUNK):
            flip(c * CHUNK + r)
        return carry

    def couple(vec):
        rows = jnp.zeros((8, KB), F32)
        for b in range(4):
            rows = jnp.where(prow_col == b, vec[b : b + 1], rows)
        mirrored = jnp.zeros((8, KB), F32)
        for k in range(PAIRS):
            mirrored = mirrored + dot(jnp.where((rows_wide & 3) == k, rows, 0.0).astype(BF16), covis[k])
        return mirrored

    def couple_rows(cols):
        out = jnp.zeros((8, KB), F32)
        for k in range(PAIRS):
            lhs = jnp.where((rows_wide & 3) == prow_ref[k], cols[k : k + 1], 0.0).astype(BF16)
            out = out + dot(lhs, covis[k], NT)
        return out

    def backward(values, start):
        out = start
        for g in range(TILES // 8):
            here = jnp.concatenate([values[32 * j + 8 * g : 32 * j + 8 * g + 8] for j in range(3)], axis=1)
            for r in range(8):
                lhs = jnp.where((rows_tq & 3) == blk_ref[g * 8 + r], here[r : r + 1], 0.0).astype(BF16)
                out = out - dot(lhs, flipped[g * 8 + r])
        return out

    def points(sums):
        parts = []
        for a in range(3):
            part = jnp.zeros((16, 128), F32)
            for e in range(3):
                part = part + inv_ref[3 * a + e] * sums[16 * e : 16 * e + 16]
            parts.append(part)
        return jnp.concatenate(parts, axis=0)

    def owners(sums_recv, src, dst, sem, own_quad):
        sums = dot(gather_rows[...], sums_recv[...])
        values = points(sums)
        inner = triple(own_quad - jnp.sum(sums * values, axis=0, keepdims=True))
        fill = jnp.concatenate([values, inner, jnp.zeros((72, 128), F32)], axis=0).astype(BF16)
        src[...] = dot(scatter_rows[...], fill).astype(BF16)
        dst[mine, :] = src[mine, :]
        exchange_all(src, dst, sem)

    def quad_row(wide_rows):
        rows = sum(wide_rows[:, 128 * j : 128 * j + 128] for j in range(6))
        return jnp.sum(rows, axis=0, keepdims=True)

    def scalars(*values):
        row = jnp.zeros((1, 128), F32)
        for k, value in enumerate(values):
            row = jnp.where(lane == k, value, row)
        return triple(row)

    def sum_trk(local, mir, values, src, dst, sem):
        quads = values[96:97] + values[97:98] + values[98:99]
        quads = jnp.where(lane == 0, jnp.sum(quads, axis=1, keepdims=True), 0.0)
        inners = mir[24:25] + mir[25:26] + mir[26:27] + quads
        src[...] = with_rows(pack(local) + mir[:24], jnp.where(sub8 == 0, inners, 0.0))
        for j in (2, 1, 3):
            remote(src, dst.at[trk], sem, (me, trk ^ j))
        dst[trk] = src[...]
        wait_rows(dst, TRKS - 1, recv_sem.at[sem])
        return (dst[0] + dst[1]) + (dst[2] + dst[3])

    forward(first, True)
    send_sums(send_sum.at[0], recv_sum.at[0], 2)

    gather_relay(recv_vec.at[0], 0)
    small[-1].wait()
    load_pairs.wait()
    mirrored = couple(first)
    inner = scalars(0.0, 0.125 * total(grad * first))
    gather_start(with_rows(pack(mirrored), inner).astype(BF16), send_mir.at[0], recv_mir.at[0], 3)
    gather_end(recv_vec.at[0], 0)
    got = recv_vec[0]
    cols = unstack(dot(pick_cols[...], got), 8, 6)
    select = iota((64, 1), 0)
    source = jnp.where(select < 32, (select & 1) * 512 + (select >> 1) * 32 + 24, (select & 31) * 32 + 25)
    tables = dot(hot(iota((64, 1024), 1) == source), got)
    mine4 = dot(tables[:32].astype(BF16), hot(iota((128, 128), 0) == me * 4 + (iota((128, 128), 1) & 3)))
    row_codes, col_codes = [], []
    sub32, lane32x = iota((32, 128), 0), iota((32, 128), 1)
    chunk = (lane >> 2) & 3
    for q in range(4):
        value = jnp.sum(jnp.where(sub32 == 8 * q + (lane32x >> 4), mine4, 0.0), axis=0, keepdims=True)
        code = jnp.where((value > 0.0) & (chunk < 3), chunk.astype(F32) * 16.0 + value - 1.0, -1.0)
        row_codes.append(code)
        code = jnp.where((chunk == 3) & ((lane & 3) < 3), 48.0 + (lane & 3).astype(F32), code)
        col_codes.append(to_col(code))
    gather_rows[...] = hot(iota((48, 512), 0).astype(F32) == jnp.concatenate(row_codes, axis=1))
    scatter_rows[...] = hot(iota((512, 128), 1).astype(F32) == jnp.concatenate(col_codes, axis=0))
    mir_codes = []
    part = (lane >> 2) & 7
    for q in range(8):
        value = jnp.sum(jnp.where(sub32 == 4 * q + (lane32x >> 5), tables[32:], 0.0), axis=0, keepdims=True)
        local = value - (me * 4).astype(F32)
        code = jnp.where((local >= 0.0) & (local < 4.0), part.astype(F32) * 4.0 + local, -1.0)
        mir_codes.append(jnp.where(part < 6, code, (lane & 31).astype(F32)))
    add_mir[...] = hot(iota((32, 1024), 0).astype(F32) == jnp.concatenate(mir_codes, axis=1))

    own_quad = quad_row(cols * mirrored + 0.125 * first * diag * first)

    wait_rows(recv_sum.at[0], 496, recv_sem.at[2])
    owners(recv_sum.at[0], send_val.at[0], recv_val.at[0], 5, own_quad)
    gather_relay(recv_mir.at[0], 3)
    coupled = couple_rows(cols)
    lax.fori_loop(0, TILES // CHUNK, flip_late, 0)
    gather_end(recv_mir.at[0], 3)
    mir = dot(add_mir[...], recv_mir[0])
    wait_rows(recv_val.at[0], 496, recv_sem.at[5])
    values = dot(from_slots[...], recv_val[0])
    local = backward(values, coupled)
    summed = sum_trk(local, mir, values, send_tot.at[0], recv_tot.at[0], 6)
    image = diag * first + unpack(summed[:24])
    dim, rz = summed[24:25, 0:1], summed[24:25, 1:2]
    alpha = rz / dim
    residual = grad - alpha * image

    vec = prec * residual
    gather_start(with_rows(pack(vec), jnp.zeros((8, 128), F32)).astype(BF16), send_vec.at[1], recv_vec.at[1], 7)
    forward(vec, False)
    send_sums(send_sum.at[1], recv_sum.at[1], 9)

    gather_relay(recv_vec.at[1], 7)
    mirrored = couple(vec)
    inner = scalars(0.0, 0.125 * total(residual * vec), 0.125 * total(vec * image))
    gather_start(with_rows(pack(mirrored), inner).astype(BF16), send_mir.at[1], recv_mir.at[1], 10)
    gather_end(recv_vec.at[1], 7)
    cols = unstack(dot(pick_cols[...], recv_vec[1]), 8, 6)
    own_quad = quad_row(cols * mirrored + 0.125 * vec * diag * vec)

    wait_rows(recv_sum.at[1], 496, recv_sem.at[9])
    owners(recv_sum.at[1], send_val.at[1], recv_val.at[1], 12, own_quad)
    gather_relay(recv_mir.at[1], 10)
    coupled = couple_rows(cols)
    gather_end(recv_mir.at[1], 10)
    mir = dot(add_mir[...], recv_mir[1])
    wait_rows(recv_val.at[1], 496, recv_sem.at[12])
    values = dot(from_slots[...], recv_val[1])
    local = backward(values, coupled)
    summed = sum_trk(local, mir, values, send_tot.at[1], recv_tot.at[1], 13)
    inners = summed[24:25]
    fresh, cross = inners[:, 1:2], inners[:, 2:3]
    beta = fresh / rz
    second = diag * vec + unpack(summed[:24]) + beta * image
    curve = inners[:, 0:1] + beta * (2.0 * cross + beta * dim)
    alpha_next = fresh / curve
    step = alpha * first + alpha_next * (vec + beta * first)
    both_ref[...] = jnp.where(iota((8, KB), 0) < 4, step, residual - alpha_next * second)

    for it in range(2):
        at = 7 * it
        wait_rows(recv_vec.at[it], 480, send_sem.at[at])
        wait_rows(recv_vec.at[it], 512, send_sem.at[at + 1])
        wait_rows(recv_sum.at[it], 496, send_sem.at[at + 2])
        wait_rows(recv_mir.at[it], 480, send_sem.at[at + 3])
        wait_rows(recv_mir.at[it], 512, send_sem.at[at + 4])
        wait_rows(recv_val.at[it], 496, send_sem.at[at + 5])
        wait_rows(recv_tot.at[it], TRKS - 1, send_sem.at[at + 6])


def shards(*args):
    args = args[:3] + (jnp.transpose(args[3], (1, 0, 2)),) + args[4:]
    vmem = pl.BlockSpec(memory_space=pltpu.VMEM)
    hbm = pl.BlockSpec(memory_space=pl.ANY)
    out = jax.ShapeDtypeStruct((8, KB), F32)
    vec = pltpu.VMEM((4, KB), F32)
    both = pl.pallas_call(
        kernel,
        out_shape=out,
        in_specs=[hbm] * 12,
        out_specs=vmem,
        scratch_shapes=[
            pltpu.VMEM((TILES, KB, TQ), BF16),
            pltpu.VMEM((TILES, TQ, KB), BF16),
            pltpu.VMEM((PAIRS, KB, KB), BF16),
            vec,
            vec,
            vec,
            pltpu.VMEM((9, 16, 128), F32),
            pltpu.SMEM((TILES,), I32),
            pltpu.SMEM((TILES,), I32),
            pltpu.SMEM((TILES,), I32),
            pltpu.SMEM((1,), I32),
            pltpu.SMEM((PAIRS,), I32),
            pltpu.SMEM((PAIRS,), I32),
            pltpu.VMEM((32, KB), F32),
            pltpu.VMEM((128, 128), F32),
            pltpu.VMEM((2, 32, 128), BF16),
            pltpu.VMEM((2, 1024, 128), BF16),
            pltpu.VMEM((2, 32, 128), BF16),
            pltpu.VMEM((2, 1024, 128), BF16),
            pltpu.VMEM((2, 512, 128), BF16),
            pltpu.VMEM((2, 512, 128), BF16),
            pltpu.VMEM((2, 512, 128), BF16),
            pltpu.VMEM((2, 512, 128), BF16),
            pltpu.VMEM((2, 32, 128), F32),
            pltpu.VMEM((2, TRKS, 32, 128), F32),
            pltpu.VMEM((512, 128), BF16),
            pltpu.VMEM((128, 512), BF16),
            pltpu.VMEM((48, 512), BF16),
            pltpu.VMEM((512, 128), BF16),
            pltpu.VMEM((48, 1024), BF16),
            pltpu.VMEM((32, 1024), BF16),
            pltpu.SemaphoreType.DMA((10,)),
            pltpu.SemaphoreType.DMA((TILES // CHUNK,)),
            pltpu.SemaphoreType.DMA,
            pltpu.SemaphoreType.DMA((14,)),
            pltpu.SemaphoreType.DMA((14,)),
        ],
        compiler_params=pltpu.CompilerParams(
            collective_id=1, has_side_effects=True, vmem_limit_bytes=56 * 2**20
        ),
        cost_estimate=pl.CostEstimate(flops=300_000_000, bytes_accessed=19_000_000, transcendentals=0),
        name="cg",
    )(*args)
    return both[:4], both[4:]


def solution(mesh):
    vec, both = P("cam", None), ("cam", "trk")
    tile, line = P(both, None, None), P(both)
    in_specs = (vec, vec, vec, tile, tile, line, line, line, line, tile, line, line)
    return jax.shard_map(shards, mesh=mesh, in_specs=in_specs, out_specs=(vec, vec), check_vma=False)
```

time: 59.7 us -> 50.3 us (0.84)
  Pallas kernels: 55.5 us -> 47.2 us
  local copies, waits for them, and re-layouts: 2.61 us -> 1.42 us
    pallas_call x1, Pallas kernels: 55.5 us -> 47.2 us  [shards(): pl.pallas_call(kernel, out_shape=out, in_specs=[hbm] * 12, out_specs=vmem...]
    unnamed x2 -> x0, local copies, waits for them, and re-layouts: 2.61 us -> none
    slice x0 -> x1, local copies, waits for them, and re-layouts: none -> 1.42 us  [shards(): return (both[:4], both[4:])]
where the time goes in v2:
time: 50.3 us; the launch traced here: 50 us
  Pallas kernels  47.2 us (94%)
  local copies, waits for them, and re-layouts  1.42 us (3%)
  between operations  1.29 us (3%)
    pallas_call x1, Pallas kernels, shards(): pl.pallas_call(kernel, out_shape=out, in_specs=[hbm] * 12, out_specs=vmem...  47.2 us
    slice x1, local copies, waits for them, and re-layouts, shards(): return (both[:4], both[4:])  1.42 us

profile of v2, /device:TPU:1, one launch (start us, length us, event | category | flops | bytes accessed | tf_op | source)
XLA Modules:
  0.0 50.0 jit_solution(17634664429034462081)
XLA Ops:
  1.3 47.2 %cg.1 = f32[8,768]{1,0:T(8,128)} custom-call(f32[4,768]{1,0:T(4,128)} %grad_hbm.1, f32[4,768]{1,0:T(4,128)} %diag_hbm.1, f32[4,768]{1,0:T(4,128)} %prec_hbm.1, f32[9,16,128]{2,1,0:T(8,128)} %bitcast.1, bf16[24,768,384]{2,1,0:T(8,128)(2,1)} %tiles_hbm.1, s32[24]{0:T(128)} %blk_hbm.1, s32[24]{0:T(128)} %own_hbm.1, s32[24]{0:T(128)} %trk_hbm.1, ...), custom_call_target="tpu_custom_call" | custom-call | flops 300000000 | bytes 19000000 | tf_op jit(solution)/shard_map/cg/pallas_call | solution.py:438
  48.5 1.4 %fusion = (f32[4,768]{1,0:T(4,128)}, f32[4,768]{1,0:T(4,128)}) fusion(f32[8,768]{1,0:T(8,128)} %cg.1), kind=kLoop, calls=%fused_computation | loop fusion | bytes 49152 | tf_op jit(solution)/shard_map/slice | solution.py:487

commit v3 on v2

--- a/solution.py
+++ b/solution.py
@@ -14,7 +14,7 @@
 KB = 768
 TQ = 384
 CHUNK = 4
-EARLY = 3
+EARLY, MID, LATE = 3, 3, 3
 NN = (((1,), (0,)), ((), ()))
 NT = (((1,), (1,)), ((), ()))
 
@@ -90,7 +90,7 @@
             )
         )
     ]
-    for copy in small:
+    for copy in small[:-1]:
         copy.start()
 
     def load_chunk(c):
@@ -98,9 +98,6 @@
         return pltpu.make_async_copy(tiles_hbm.at[part], tiles.at[part], tile_sem.at[c])
 
     load_pairs = pltpu.make_async_copy(covis_hbm, covis, covis_sem)
-    for c in range(TILES // CHUNK):
-        load_chunk(c).start()
-    load_pairs.start()
 
     barrier = pltpu.get_barrier_semaphore()
 
@@ -115,6 +112,10 @@
     lax.fori_loop(0, CAMS - 1, greet, 0)
     for j in range(1, TRKS):
         pl.semaphore_signal(barrier, inc=1, device_id=(me, trk ^ j), device_id_type=MESH)
+    for c in range(TILES // CHUNK):
+        load_chunk(c).start()
+    small[-1].start()
+    load_pairs.start()
 
     def remote(src, dst, sem, to):
         pltpu.make_async_remote_copy(
@@ -263,10 +264,16 @@
     def flip(i):
         flipped[i] = tiles[i].T
 
-    def flip_late(c, carry):
-        for r in range(EARLY, CHUNK):
-            flip(c * CHUNK + r)
-        return carry
+    chunks = TILES // CHUNK
+    left = TILES - chunks * EARLY
+
+    def flip_left(start, end):
+        def one(k, carry):
+            flip((k % chunks) * CHUNK + EARLY + k // chunks)
+            return carry
+
+        if start < end:
+            lax.fori_loop(start, end, one, 0)
 
     def couple(vec):
         rows = jnp.zeros((8, KB), F32)
@@ -284,13 +291,16 @@
             out = out + dot(lhs, covis[k], NT)
         return out
 
-    def backward(values, start):
+    def backward(values, start, done):
         out = start
         for g in range(TILES // 8):
             here = jnp.concatenate([values[32 * j + 8 * g : 32 * j + 8 * g + 8] for j in range(3)], axis=1)
             for r in range(8):
                 lhs = jnp.where((rows_tq & 3) == blk_ref[g * 8 + r], here[r : r + 1], 0.0).astype(BF16)
-                out = out - dot(lhs, flipped[g * 8 + r])
+                if (r % CHUNK - EARLY) * chunks + (g * 8 + r) // CHUNK < done:
+                    out = out - dot(lhs, flipped[g * 8 + r])
+                else:
+                    out = out - dot(lhs, tiles[g * 8 + r], NT)
         return out
 
     def points(sums):
@@ -321,7 +331,7 @@
             row = jnp.where(lane == k, value, row)
         return triple(row)
 
-    def sum_trk(local, mir, values, src, dst, sem):
+    def sum_trk(local, mir, values, src, dst, sem, meanwhile):
         quads = values[96:97] + values[97:98] + values[98:99]
         quads = jnp.where(lane == 0, jnp.sum(quads, axis=1, keepdims=True), 0.0)
         inners = mir[24:25] + mir[25:26] + mir[26:27] + quads
@@ -329,6 +339,7 @@
         for j in (2, 1, 3):
             remote(src, dst.at[trk], sem, (me, trk ^ j))
         dst[trk] = src[...]
+        meanwhile()
         wait_rows(dst, TRKS - 1, recv_sem.at[sem])
         return (dst[0] + dst[1]) + (dst[2] + dst[3])
 
@@ -370,17 +381,18 @@
 
     own_quad = quad_row(cols * mirrored + 0.125 * first * diag * first)
 
+    flip_left(0, MID)
     wait_rows(recv_sum.at[0], 496, recv_sem.at[2])
     owners(recv_sum.at[0], send_val.at[0], recv_val.at[0], 5, own_quad)
     gather_relay(recv_mir.at[0], 3)
     coupled = couple_rows(cols)
-    lax.fori_loop(0, TILES // CHUNK, flip_late, 0)
+    flip_left(MID, MID + LATE)
     gather_end(recv_mir.at[0], 3)
     mir = dot(add_mir[...], recv_mir[0])
     wait_rows(recv_val.at[0], 496, recv_sem.at[5])
     values = dot(from_slots[...], recv_val[0])
-    local = backward(values, coupled)
-    summed = sum_trk(local, mir, values, send_tot.at[0], recv_tot.at[0], 6)
+    local = backward(values, coupled, MID + LATE)
+    summed = sum_trk(local, mir, values, send_tot.at[0], recv_tot.at[0], 6, lambda: flip_left(MID + LATE, left))
     image = diag * first + unpack(summed[:24])
     dim, rz = summed[24:25, 0:1], summed[24:25, 1:2]
     alpha = rz / dim
@@ -407,8 +419,8 @@
     mir = dot(add_mir[...], recv_mir[1])
     wait_rows(recv_val.at[1], 496, recv_sem.at[12])
     values = dot(from_slots[...], recv_val[1])
-    local = backward(values, coupled)
-    summed = sum_trk(local, mir, values, send_tot.at[1], recv_tot.at[1], 13)
+    local = backward(values, coupled, left)
+    summed = sum_trk(local, mir, values, send_tot.at[1], recv_tot.at[1], 13, lambda: None)
     inners = summed[24:25]
     fresh, cross = inners[:, 1:2], inners[:, 2:3]
     beta = fresh / rz

time: 50.3 us -> 49.8 us (0.990)
  no operation moved by 1% of the time
where the time goes in v3:
time: 49.8 us; the launch traced here: 49.6 us
  Pallas kernels  46.9 us (94%)
  local copies, waits for them, and re-layouts  1.42 us (3%)
  between operations  1.29 us (3%)
    pallas_call x1, Pallas kernels, shards(): pl.pallas_call(kernel, out_shape=out, in_specs=[hbm] * 12, out_specs=vmem...  46.9 us
    slice x1, local copies, waits for them, and re-layouts, shards(): return (both[:4], both[4:])  1.42 us

profile of v3, /device:TPU:1, one launch (start us, length us, event | category | flops | bytes accessed | tf_op | source)
XLA Modules:
  0.0 49.6 jit_solution(8640060370485130598)
XLA Ops:
  1.3 46.9 %cg.1 = f32[8,768]{1,0:T(8,128)} custom-call(f32[4,768]{1,0:T(4,128)} %grad_hbm.1, f32[4,768]{1,0:T(4,128)} %diag_hbm.1, f32[4,768]{1,0:T(4,128)} %prec_hbm.1, f32[9,16,128]{2,1,0:T(8,128)} %bitcast.1, bf16[24,768,384]{2,1,0:T(8,128)(2,1)} %tiles_hbm.1, s32[24]{0:T(128)} %blk_hbm.1, s32[24]{0:T(128)} %own_hbm.1, s32[24]{0:T(128)} %trk_hbm.1, ...), custom_call_target="tpu_custom_call" | custom-call | flops 300000000 | bytes 19000000 | tf_op jit(solution)/shard_map/cg/pallas_call | solution.py:450
  48.2 1.4 %fusion = (f32[4,768]{1,0:T(4,128)}, f32[4,768]{1,0:T(4,128)}) fusion(f32[8,768]{1,0:T(8,128)} %cg.1), kind=kLoop, calls=%fused_computation | loop fusion | bytes 49152 | tf_op jit(solution)/shard_map/slice | solution.py:499

commit v4 on v2

--- a/solution.py
+++ b/solution.py
@@ -68,6 +68,7 @@
     tiles, flipped, covis, grad_ref, diag_ref, prec_ref, inv_ref, blk_ref, own_ref, trk_ref, live_ref, prow_ref, pcol_ref,
     wide, stack, send_vec, recv_vec, send_mir, recv_mir, send_sum, recv_sum, send_val, recv_val,
     send_tot, recv_tot, to_slots, from_slots, gather_rows, scatter_rows, pick_cols, add_mir,
+    vec_now, residual_now, image_now, total_now, inners_first, points_now,
     load_sem, tile_sem, covis_sem, send_sem, recv_sem,
 ):
     me, trk = lax.axis_index("cam"), lax.axis_index("trk")
@@ -90,7 +91,7 @@
             )
         )
     ]
-    for copy in small:
+    for copy in small[:-1]:
         copy.start()
 
     def load_chunk(c):
@@ -98,9 +99,6 @@
         return pltpu.make_async_copy(tiles_hbm.at[part], tiles.at[part], tile_sem.at[c])
 
     load_pairs = pltpu.make_async_copy(covis_hbm, covis, covis_sem)
-    for c in range(TILES // CHUNK):
-        load_chunk(c).start()
-    load_pairs.start()
 
     barrier = pltpu.get_barrier_semaphore()
 
@@ -115,6 +113,10 @@
     lax.fori_loop(0, CAMS - 1, greet, 0)
     for j in range(1, TRKS):
         pl.semaphore_signal(barrier, inc=1, device_id=(me, trk ^ j), device_id_type=MESH)
+    for c in range(TILES // CHUNK):
+        load_chunk(c).start()
+    small[-1].start()
+    load_pairs.start()
 
     def remote(src, dst, sem, to):
         pltpu.make_async_remote_copy(
@@ -263,9 +265,10 @@
     def flip(i):
         flipped[i] = tiles[i].T
 
-    def flip_late(c, carry):
-        for r in range(EARLY, CHUNK):
-            flip(c * CHUNK + r)
+    late = CHUNK - EARLY
+
+    def flip_late(k, carry):
+        flip((k // late) * CHUNK + EARLY + k % late)
         return carry
 
     def couple(vec):
@@ -285,13 +288,18 @@
         return out
 
     def backward(values, start):
-        out = start
-        for g in range(TILES // 8):
-            here = jnp.concatenate([values[32 * j + 8 * g : 32 * j + 8 * g + 8] for j in range(3)], axis=1)
+        points_now[...] = values
+
+        def group(g, out):
+            here = jnp.concatenate(
+                [points_now[pl.ds(pl.multiple_of(32 * j + 8 * g, 8), 8), :] for j in range(3)], axis=1
+            )
             for r in range(8):
                 lhs = jnp.where((rows_tq & 3) == blk_ref[g * 8 + r], here[r : r + 1], 0.0).astype(BF16)
                 out = out - dot(lhs, flipped[g * 8 + r])
-        return out
+            return out
+
+        return lax.fori_loop(0, TILES // 8, group, start)
 
     def points(sums):
         parts = []
@@ -332,83 +340,102 @@
         wait_rows(dst, TRKS - 1, recv_sem.at[sem])
         return (dst[0] + dst[1]) + (dst[2] + dst[3])
 
-    forward(first, True)
-    send_sums(send_sum.at[0], recv_sum.at[0], 2)
-
-    gather_relay(recv_vec.at[0], 0)
-    small[-1].wait()
-    load_pairs.wait()
-    mirrored = couple(first)
-    inner = scalars(0.0, 0.125 * total(grad * first))
-    gather_start(with_rows(pack(mirrored), inner).astype(BF16), send_mir.at[0], recv_mir.at[0], 3)
-    gather_end(recv_vec.at[0], 0)
-    got = recv_vec[0]
-    cols = unstack(dot(pick_cols[...], got), 8, 6)
-    select = iota((64, 1), 0)
-    source = jnp.where(select < 32, (select & 1) * 512 + (select >> 1) * 32 + 24, (select & 31) * 32 + 25)
-    tables = dot(hot(iota((64, 1024), 1) == source), got)
-    mine4 = dot(tables[:32].astype(BF16), hot(iota((128, 128), 0) == me * 4 + (iota((128, 128), 1) & 3)))
-    row_codes, col_codes = [], []
-    sub32, lane32x = iota((32, 128), 0), iota((32, 128), 1)
-    chunk = (lane >> 2) & 3
-    for q in range(4):
-        value = jnp.sum(jnp.where(sub32 == 8 * q + (lane32x >> 4), mine4, 0.0), axis=0, keepdims=True)
-        code = jnp.where((value > 0.0) & (chunk < 3), chunk.astype(F32) * 16.0 + value - 1.0, -1.0)
-        row_codes.append(code)
-        code = jnp.where((chunk == 3) & ((lane & 3) < 3), 48.0 + (lane & 3).astype(F32), code)
-        col_codes.append(to_col(code))
-    gather_rows[...] = hot(iota((48, 512), 0).astype(F32) == jnp.concatenate(row_codes, axis=1))
-    scatter_rows[...] = hot(iota((512, 128), 1).astype(F32) == jnp.concatenate(col_codes, axis=0))
-    mir_codes = []
-    part = (lane >> 2) & 7
-    for q in range(8):
-        value = jnp.sum(jnp.where(sub32 == 4 * q + (lane32x >> 5), tables[32:], 0.0), axis=0, keepdims=True)
-        local = value - (me * 4).astype(F32)
-        code = jnp.where((local >= 0.0) & (local < 4.0), part.astype(F32) * 4.0 + local, -1.0)
-        mir_codes.append(jnp.where(part < 6, code, (lane & 31).astype(F32)))
-    add_mir[...] = hot(iota((32, 1024), 0).astype(F32) == jnp.concatenate(mir_codes, axis=1))
-
-    own_quad = quad_row(cols * mirrored + 0.125 * first * diag * first)
-
-    wait_rows(recv_sum.at[0], 496, recv_sem.at[2])
-    owners(recv_sum.at[0], send_val.at[0], recv_val.at[0], 5, own_quad)
-    gather_relay(recv_mir.at[0], 3)
-    coupled = couple_rows(cols)
-    lax.fori_loop(0, TILES // CHUNK, flip_late, 0)
-    gather_end(recv_mir.at[0], 3)
-    mir = dot(add_mir[...], recv_mir[0])
-    wait_rows(recv_val.at[0], 496, recv_sem.at[5])
-    values = dot(from_slots[...], recv_val[0])
-    local = backward(values, coupled)
-    summed = sum_trk(local, mir, values, send_tot.at[0], recv_tot.at[0], 6)
-    image = diag * first + unpack(summed[:24])
-    dim, rz = summed[24:25, 0:1], summed[24:25, 1:2]
+    def make_tables():
+        got = recv_vec[0]
+        select = iota((64, 1), 0)
+        source = jnp.where(select < 32, (select & 1) * 512 + (select >> 1) * 32 + 24, (select & 31) * 32 + 25)
+        tables = dot(hot(iota((64, 1024), 1) == source), got)
+        mine4 = dot(tables[:32].astype(BF16), hot(iota((128, 128), 0) == me * 4 + (iota((128, 128), 1) & 3)))
+        row_codes, col_codes = [], []
+        sub32, lane32x = iota((32, 128), 0), iota((32, 128), 1)
+        chunk = (lane >> 2) & 3
+        for q in range(4):
+            value = jnp.sum(jnp.where(sub32 == 8 * q + (lane32x >> 4), mine4, 0.0), axis=0, keepdims=True)
+            code = jnp.where((value > 0.0) & (chunk < 3), chunk.astype(F32) * 16.0 + value - 1.0, -1.0)
+            row_codes.append(code)
+            code = jnp.where((chunk == 3) & ((lane & 3) < 3), 48.0 + (lane & 3).astype(F32), code)
+            col_codes.append(to_col(code))
+        gather_rows[...] = hot(iota((48, 512), 0).astype(F32) == jnp.concatenate(row_codes, axis=1))
+        scatter_rows[...] = hot(iota((512, 128), 1).astype(F32) == jnp.concatenate(col_codes, axis=0))
+        mir_codes = []
+        part = (lane >> 2) & 7
+        for q in range(8):
+            value = jnp.sum(jnp.where(sub32 == 4 * q + (lane32x >> 5), tables[32:], 0.0), axis=0, keepdims=True)
+            local = value - (me * 4).astype(F32)
+            code = jnp.where((local >= 0.0) & (local < 4.0), part.astype(F32) * 4.0 + local, -1.0)
+            mir_codes.append(jnp.where(part < 6, code, (lane & 31).astype(F32)))
+        add_mir[...] = hot(iota((32, 1024), 0).astype(F32) == jnp.concatenate(mir_codes, axis=1))
+
+
+    def application(it, carry):
+        at = 7 * it
+        vec = vec_now[...]
+        pl.when(it == 0)(lambda: forward(vec, True))
+        pl.when(it == 1)(lambda: forward(vec, False))
+        send_sums(send_sum.at[it], recv_sum.at[it], at + 2)
+
+        gather_relay(recv_vec.at[it], at)
+
+        @pl.when(it == 0)
+        def _():
+            small[-1].wait()
+            load_pairs.wait()
+
+        mirrored = couple(vec)
+        inner = scalars(0.0, 0.125 * total(residual_now[...] * vec), 0.125 * total(vec * image_now[...]))
+        gather_start(with_rows(pack(mirrored), inner).astype(BF16), send_mir.at[it], recv_mir.at[it], at + 3)
+        gather_end(recv_vec.at[it], at)
+        pl.when(it == 0)(make_tables)
+        cols = unstack(dot(pick_cols[...], recv_vec[it]), 8, 6)
+        own_quad = quad_row(cols * mirrored + 0.125 * vec * diag * vec)
+
+        @pl.when(it == 0)
+        def _():
+            lax.fori_loop(0, 3, flip_late, 0)
+
+        wait_rows(recv_sum.at[it], 496, recv_sem.at[at + 2])
+        owners(recv_sum.at[it], send_val.at[it], recv_val.at[it], at + 5, own_quad)
+        gather_relay(recv_mir.at[it], at + 3)
+        coupled = couple_rows(cols)
+
+        @pl.when(it == 0)
+        def _():
+            lax.fori_loop(3, TILES // CHUNK * late, flip_late, 0)
+
+        gather_end(recv_mir.at[it], at + 3)
+        mir = dot(add_mir[...], recv_mir[it])
+        wait_rows(recv_val.at[it], 496, recv_sem.at[at + 5])
+        values = dot(from_slots[...], recv_val[it])
+        local = backward(values, coupled)
+        summed = sum_trk(local, mir, values, send_tot.at[it], recv_tot.at[it], at + 6)
+
+        @pl.when(it == 0)
+        def _():
+            image = diag * vec + unpack(summed[:24])
+            residual = grad - (summed[24:25, 1:2] / summed[24:25, 0:1]) * image
+            after = prec * residual
+            gather_start(
+                with_rows(pack(after), jnp.zeros((8, 128), F32)).astype(BF16), send_vec.at[1], recv_vec.at[1], 7
+            )
+            vec_now[...] = after
+            image_now[...] = image
+            residual_now[...] = residual
+            inners_first[...] = summed[24:32]
+
+        @pl.when(it == 1)
+        def _():
+            total_now[...] = summed
+
+        return carry
+
+    vec_now[...] = first
+    residual_now[...] = grad
+    image_now[...] = jnp.zeros((8, KB), F32)
+    lax.fori_loop(0, 2, application, 0)
+
+    vec, image, residual, summed = vec_now[...], image_now[...], residual_now[...], total_now[...]
+    dim, rz = inners_first[0:1, 0:1], inners_first[0:1, 1:2]
     alpha = rz / dim
-    residual = grad - alpha * image
-
-    vec = prec * residual
-    gather_start(with_rows(pack(vec), jnp.zeros((8, 128), F32)).astype(BF16), send_vec.at[1], recv_vec.at[1], 7)
-    forward(vec, False)
-    send_sums(send_sum.at[1], recv_sum.at[1], 9)
-
-    gather_relay(recv_vec.at[1], 7)
-    mirrored = couple(vec)
-    inner = scalars(0.0, 0.125 * total(residual * vec), 0.125 * total(vec * image))
-    gather_start(with_rows(pack(mirrored), inner).astype(BF16), send_mir.at[1], recv_mir.at[1], 10)
-    gather_end(recv_vec.at[1], 7)
-    cols = unstack(dot(pick_cols[...], recv_vec[1]), 8, 6)
-    own_quad = quad_row(cols * mirrored + 0.125 * vec * diag * vec)
-
-    wait_rows(recv_sum.at[1], 496, recv_sem.at[9])
-    owners(recv_sum.at[1], send_val.at[1], recv_val.at[1], 12, own_quad)
-    gather_relay(recv_mir.at[1], 10)
-    coupled = couple_rows(cols)
-    gather_end(recv_mir.at[1], 10)
-    mir = dot(add_mir[...], recv_mir[1])
-    wait_rows(recv_val.at[1], 496, recv_sem.at[12])
-    values = dot(from_slots[...], recv_val[1])
-    local = backward(values, coupled)
-    summed = sum_trk(local, mir, values, send_tot.at[1], recv_tot.at[1], 13)
     inners = summed[24:25]
     fresh, cross = inners[:, 1:2], inners[:, 2:3]
     beta = fresh / rz
@@ -472,6 +499,12 @@
             pltpu.VMEM((512, 128), BF16),
             pltpu.VMEM((48, 1024), BF16),
             pltpu.VMEM((32, 1024), BF16),
+            pltpu.VMEM((8, KB), F32),
+            pltpu.VMEM((8, KB), F32),
+            pltpu.VMEM((8, KB), F32),
+            pltpu.VMEM((32, 128), F32),
+            pltpu.VMEM((8, 128), F32),
+            pltpu.VMEM((128, 128), F32),
             pltpu.SemaphoreType.DMA((10,)),
             pltpu.SemaphoreType.DMA((TILES // CHUNK,)),
             pltpu.SemaphoreType.DMA,

time: 50.3 us -> 50 us (level)
  no operation moved by 1% of the time
where the time goes in v4:
time: 50 us; the launch traced here: 49.8 us
  Pallas kernels  47.1 us (94%)
  local copies, waits for them, and re-layouts  1.42 us (3%)
  between operations  1.29 us (3%)
    pallas_call x1, Pallas kernels, shards(): pl.pallas_call(kernel, out_shape=out, in_specs=[hbm] * 12, out_specs=vmem...  47.1 us
    slice x1, local copies, waits for them, and re-layouts, shards(): return (both[:4], both[4:])  1.42 us

profile of v4, /device:TPU:1, one launch (start us, length us, event | category | flops | bytes accessed | tf_op | source)
XLA Modules:
  0.0 49.8 jit_solution(13194596394772864679)
XLA Ops:
  1.3 47.1 %cg.1 = f32[8,768]{1,0:T(8,128)} custom-call(f32[4,768]{1,0:T(4,128)} %grad_hbm.1, f32[4,768]{1,0:T(4,128)} %diag_hbm.1, f32[4,768]{1,0:T(4,128)} %prec_hbm.1, f32[9,16,128]{2,1,0:T(8,128)} %bitcast.1, bf16[24,768,384]{2,1,0:T(8,128)(2,1)} %tiles_hbm.1, s32[24]{0:T(128)} %blk_hbm.1, s32[24]{0:T(128)} %own_hbm.1, s32[24]{0:T(128)} %trk_hbm.1, ...), custom_call_target="tpu_custom_call" | custom-call | flops 300000000 | bytes 19000000 | tf_op jit(solution)/shard_map/cg/pallas_call | solution.py:465
  48.4 1.4 %fusion = (f32[4,768]{1,0:T(4,128)}, f32[4,768]{1,0:T(4,128)}) fusion(f32[8,768]{1,0:T(8,128)} %cg.1), kind=kLoop, calls=%fused_computation | loop fusion | bytes 49152 | tf_op jit(solution)/shard_map/slice | solution.py:520
